TPU v7x, 768 devices: a whole 4x8x12 slice. The times are simulated.
768 devices in a mesh: stn: 32 (over z_lo, x, core), tm: 24 (over z_hi, y).
Axes of the slice: x: 4, y: 8, z: 12 (z_hi: 3, z_lo: 4; z = z_hi * 4 + z_lo), core: 2. Of those that a mesh axis runs over, the one named last changes fastest.
Arguments:
- samples: bfloat16 [2, 64, 96, 4096], P(None, 'stn', 'tm'), may hold values from -6 to 6
- valid_spectra: int32 [24], P('tm'), may hold values from 1 to 4, as said below
- root_blocks: int32 [4], replicated, may hold values from 0 to 31, as said below
Outputs:
- visibilities: float32 [24, 2, 4, 64, 2, 4096], P('tm', None, None, 'stn')
Inputs may be any that keep to these rules, and one draw needn't show every extreme that they name: `valid_spectra`: every value from 1 to 4; some time block has exactly 4, some exactly 1. `root_blocks`: 4 different station blocks, in an order drawn from the seed; block 0 and block 32 - 1 are always among them.
All inputs are finite; a program needn't handle non-finite values.
Results may differ from a plain program's by a relative error of at most 0.004.
Values may be sent and summed in bfloat16 or wider, within the bound.
No kernel may reach another device: no remote copies, remote signals or barrier semaphores. Data moves between devices by JAX's collectives and lax.ppermute only.
A program may use at most 32 MiB of HBM per device.

v0:
```python
import math

import jax
import jax.numpy as jnp
from jax import lax
from jax.sharding import PartitionSpec as P

TAPS = 4
STEPS = 4


def passed_along(value, axis, steps):
    count = lax.axis_size(axis)
    leading, last = (max(0, -steps), min(count, count - steps))
    return lax.ppermute(value, axis, [(source, source + steps) for source in range(leading, last)])


def spread(x, axis, root):
    mine = lax.axis_index(axis) == root
    return lax.psum(jnp.where(mine, x, jnp.zeros_like(x)), axis)


def prototype(channels, taps):
    positions = jnp.arange(taps * channels, dtype=jnp.float32)
    middle = (positions - 0.5 * taps * channels + 0.5) / channels
    window = 0.5 - 0.5 * jnp.cos(2.0 * math.pi * (positions + 0.5) / (taps * channels))
    return (jnp.sinc(middle) * window).reshape(taps, channels)


def filtered(extended, taps_table, frames):
    running = jnp.zeros(extended.shape[:2] + (frames, extended.shape[3]), jnp.float32)
    for tap_index in range(taps_table.shape[0]):
        running = running + taps_table[tap_index] * extended[
            :, :, tap_index : tap_index + frames
        ].astype(jnp.float32)
    return running


def angles(left, right, period):
    product = left[:, None] * right[None, :] % period
    return 2.0 * math.pi * product.astype(jnp.float32) / period


def transform(filt, norm_scale):
    signals, frames, channels = (filt.shape[1], filt.shape[2], filt.shape[3])
    col_count = 128
    row_count = channels // col_count
    higher = lax.Precision.HIGH
    real_in = filt[0].reshape(signals, frames, row_count, col_count)
    imag_in = filt[1].reshape(signals, frames, row_count, col_count)
    row_index = jnp.arange(row_count, dtype=jnp.int32)
    col_index = jnp.arange(col_count, dtype=jnp.int32)
    row_angle = angles(row_index, row_index, row_count)
    cos_rows, sin_rows = (jnp.cos(row_angle), jnp.sin(row_angle))
    mid_real = jnp.einsum("ab,pmbn->pman", cos_rows, real_in, precision=higher) + jnp.einsum(
        "ab,pmbn->pman", sin_rows, imag_in, precision=higher
    )
    mid_imag = jnp.einsum("ab,pmbn->pman", cos_rows, imag_in, precision=higher) - jnp.einsum(
        "ab,pmbn->pman", sin_rows, real_in, precision=higher
    )
    twiddle = angles(row_index, col_index, channels)
    twist_cos, twist_sin = (jnp.cos(twiddle), jnp.sin(twiddle))
    turned_real = mid_real * twist_cos + mid_imag * twist_sin
    turned_imag = mid_imag * twist_cos - mid_real * twist_sin
    col_angle = angles(col_index, col_index, col_count)
    cos_cols, sin_cols = (jnp.cos(col_angle), jnp.sin(col_angle))
    out_real = jnp.einsum("pman,cn->pmac", turned_real, cos_cols, precision=higher) + jnp.einsum(
        "pman,cn->pmac", turned_imag, sin_cols, precision=higher
    )
    out_imag = jnp.einsum("pman,cn->pmac", turned_imag, cos_cols, precision=higher) - jnp.einsum(
        "pman,cn->pmac", turned_real, sin_cols, precision=higher
    )
    spec_real = (
        jnp.swapaxes(out_real * norm_scale, 2, 3)
        .reshape(signals, frames, channels)
        .astype(jnp.bfloat16)
    )
    spec_imag = (
        jnp.swapaxes(out_imag * norm_scale, 2, 3)
        .reshape(signals, frames, channels)
        .astype(jnp.bfloat16)
    )
    return (spec_real, spec_imag)


def local(samples, valid_spectra, root_blocks):
    signals, frames, channels = (samples.shape[1], samples.shape[2], samples.shape[3])
    taps_table = prototype(channels, TAPS)
    norm_scale = 1.0 / math.sqrt(channels)
    tail_frames = samples[:, :, frames - (TAPS - 1) :]
    history = passed_along(tail_frames, "tm", 1)
    extended = jnp.concatenate([history, samples], axis=2)
    spec_real, spec_imag = transform(filtered(extended, taps_table, frames), norm_scale)
    valid_count = valid_spectra[0]
    usable = (jnp.arange(frames) < valid_count).astype(jnp.float32)
    own_real = spec_real.astype(jnp.float32) * usable[None, :, None]
    own_imag = spec_imag.astype(jnp.float32) * usable[None, :, None]

    def fetch_block(root_block):
        remote = spread(jnp.stack([spec_real, spec_imag]), "stn", root_block)
        return (remote[0], remote[1])

    def correlate(root_block):
        far_real, far_imag = fetch_block(root_block)
        far_real = far_real.astype(jnp.float32)[None]
        far_imag = far_imag.astype(jnp.float32)[None]
        left_real = own_real[:, None]
        left_imag = own_imag[:, None]
        vis_real = jnp.sum(left_real * far_real + left_imag * far_imag, axis=2)
        vis_imag = jnp.sum(left_imag * far_real - left_real * far_imag, axis=2)
        return jnp.stack([vis_real, vis_imag]) / valid_count.astype(jnp.float32)

    result = jnp.stack([correlate(root_blocks[step_index]) for step_index in range(STEPS)], axis=1)
    return result[None]


def solution(mesh):
    return jax.shard_map(
        local,
        mesh=mesh,
        in_specs=(P(None, "stn", "tm", None), P("tm"), P()),
        out_specs=P("tm", None, None, "stn", None, None),
        check_vma=False,
    )
```

profile of v0, /device:TPU:1, one launch (start us, length us, event | category | flops | bytes accessed | tf_op | source)
XLA Modules:
  0.0 337.5 jit_solution(12053558845819971931)
XLA Ops:
  6.5 1.0 slice.71
  7.5 4.2 %collective-permute-start = (bf16[2,2,3,4096]{3,2,1,0:T(4,128)(2,1)S(1)}, bf16[2,2,3,4096]{3,2,1,0:T(4,128)(2,1)S(1)}, u32[]{:S(2)}, u32[]{:S(2)}) collective-permute-start(bf16[2,2,3,4096]{3,2,1,0:T(4,128)(2,1)S(1)} %slice.71), channel_id=1, source_target_pairs={{0,1},{1,2},{2,3},{3,4},{4,5},{5,6},{6,7},{7,8},{8,9},{9,10},{10,1... | collective-permute-start | bytes 294920 | tf_op jit(solution)/shard_map/ppermute | solution.py:15
  11.7 0.3 fusion.14
  12.0 0.1 fusion.83
  12.8 0.7 fusion.125
  16.0 0.4 multiply_add_fusion
  16.4 0.1 reshape_squeeze.6
  16.5 0.3 fusion.75
  16.8 0.1 reshape_squeeze.7
  16.9 0.3 fusion.73
  17.2 0.3 fusion.1
  17.5 0.3 fusion
  17.7 0.5 fusion.52
  18.2 0.5 fusion.54
  18.7 0.5 fusion.7
  19.2 0.1 copy.11
  19.3 0.2 copy.10
  19.5 0.5 fusion.6
  20.0 0.1 copy.8
  20.1 0.2 copy.9
  20.3 0.3 reshape.224
  20.6 0.3 reshape.222
  20.9 0.3 convert_element_type.161
  21.1 0.3 convert_element_type.158
  21.5 0.9 broadcast_select_fusion
  22.5 0.1 broadcast_multiply_fusion.1
  22.6 302.1 %all-reduce.3.cloned.1.call-done = (bf16[2,2,4,4096]{3,2,1,0:T(4,128)(2,1)}, bf16[2,2,4,4096]{3,2,1,0:T(4,128)(2,1)}, bf16[2,2,4,4096]{3,2,1,0:T(4,128)(2,1)}, bf16[2,2,4,4096]{3,2,1,0:T(4,128)(2,1)}) async-done(((bf16[2,2,4,4096]{3,2,1,0:T(4,128)(2,1)}, bf16[2,2,4,4096]{3,2,1,0:T(4,128)(2,1)}, bf16[2,2,4,4096]{3,2,1,0:T(4,128)(2,1)}, bf16[2,2,4,4096]{3,2,1,0:T(4,128)(2,1)}), ...) | async-done | bytes 524304 | tf_op jit(solution)/shard_map/psum | solution.py:20
  324.7 0.9 fusion.43
  325.7 0.9 copy-done.2
  326.6 0.9 copy-done.1
  327.5 1.8 add_reduce_fusion.3
  329.6 1.1 maximum_bitcast_fusion
  (23 shorter events, 0.5 us)
Async XLA Ops:
  6.5 318.2 %all-reduce.3.cloned.1.call-start = ((), (), s32[]{:S(2)}) async-start(), calls=%async_computation | async-start | bytes 1048576 | tf_op jit(solution)/shard_map/psum | solution.py:20
  7.5 8.5 %copy-start = (bf16[2,2,4,4096]{3,2,1,0:T(4,128)(2,1)S(1)}, bf16[2,2,4,4096]{3,2,1,0:T(4,128)(2,1)}, u32[]{:S(2)}) copy-start(bf16[2,2,4,4096]{3,2,1,0:T(4,128)(2,1)} %param.3) | copy-start | bytes 393220
  7.5 8.5 %collective-permute-start = (bf16[2,2,3,4096]{3,2,1,0:T(4,128)(2,1)S(1)}, bf16[2,2,3,4096]{3,2,1,0:T(4,128)(2,1)S(1)}, u32[]{:S(2)}, u32[]{:S(2)}) collective-permute-start(bf16[2,2,3,4096]{3,2,1,0:T(4,128)(2,1)S(1)} %slice.71), channel_id=1, source_target_pairs={{0,1},{1,2},{2,3},{3,4},{4,5},{5,6},{6,7},{7,8},{8,9},{9,10},{10,1... | collective-permute-start | bytes 294920 | tf_op jit(solution)/shard_map/ppermute | solution.py:15
  12.1 0.7 copy-start.4
  324.7 1.0 copy-start.3
  325.7 0.9 copy-start.2
  326.6 0.9 copy-start.1
Sparse Core Ops, SparseCore 0:
  22.6 302.0 all-reduce.2
where the time goes:
time: 338 us
  waiting for transfers between devices  302 us (89%)
  between operations  16.8 us (5%)
  other arithmetic  6.01 us (2%)
  local copies, waits for them, and re-layouts  5.45 us (2%)
  starting transfers between devices  4.17 us (1%)
    psum x1, waiting for transfers between devices, spread(): return lax.psum(jnp.where(mine, x, jnp.zeros_like(x)), axis)  302 us
  transfers between devices with their start and end apart: 2, of which 1 were waited for; matrix products, arithmetic and copies ran while one was open for 0% of the time, Pallas kernels for 0%

commit v1 on v0

v1 whole, which is shorter than its diff:
```python
import math

import jax
import jax.numpy as jnp
import ml_dtypes
import numpy as np
from jax import lax
from jax.experimental import pallas as pl
from jax.experimental.pallas import tpu as pltpu
from jax.sharding import PartitionSpec as P

TAPS = 4
STEPS = 4
ROWS = 32
COLS = 128
F32, BF16 = jnp.float32, jnp.bfloat16
VMEM = pl.BlockSpec(memory_space=pltpu.VMEM)
SMEM = pl.BlockSpec(memory_space=pltpu.SMEM)


def split(table):
    high = table.astype(ml_dtypes.bfloat16)
    low = (table - high.astype(np.float64)).astype(ml_dtypes.bfloat16)
    return high, low


def tables(channels):
    position = np.arange(TAPS * channels, dtype=np.float64)
    middle = (position - 0.5 * TAPS * channels + 0.5) / channels
    window = 0.5 - 0.5 * np.cos(2.0 * np.pi * (position + 0.5) / (TAPS * channels))
    taps = (np.sinc(middle) * window).astype(np.float32).reshape(TAPS * ROWS, COLS)
    row, col = np.arange(ROWS), np.arange(COLS)
    angle = 2.0 * np.pi * (row[:, None] * row[None, :] % ROWS) / ROWS
    cos, sin = np.cos(angle), np.sin(angle)
    high, low = split(np.block([[cos, sin], [-sin, cos]]))
    first = np.concatenate([high, high, low], axis=1)
    angle = 2.0 * np.pi * (row[:, None] * col[None, :]) / channels
    twist = np.concatenate([np.cos(angle), np.sin(angle)]).astype(np.float32)
    out_col = (4 * np.arange(32)[None, :] + np.arange(4)[:, None]).reshape(-1)
    angle = 2.0 * np.pi * (out_col[:, None] * col[None, :] % COLS) / COLS
    scale = 1.0 / math.sqrt(channels)
    cos, sin = np.cos(angle) * scale, np.sin(angle) * scale
    high, low = split(np.block([[cos, sin], [-sin, cos]]))
    second = np.concatenate([high, high, low], axis=1)
    return taps, first, twist, second


def spectra_kernel(own, past, taps, first, twist, second, by_tile, by_row, ext, mixed):
    for part in range(2):
        for sig in range(2):
            base = (part * 2 + sig) * ROWS * 8
            before = past[part, sig].astype(F32)
            now = own[part, sig].astype(F32)
            for tile in range(ROWS):
                lanes = slice(tile * COLS, (tile + 1) * COLS)
                ext[base + tile * 8 : base + tile * 8 + 4, :] = before[:, lanes]
                ext[base + tile * 8 + 4 : base + tile * 8 + 8, :] = now[:, lanes]
    weights = [taps[k * ROWS : (k + 1) * ROWS, :] for k in range(TAPS)]
    columns = []
    for sig in range(2):
        both = []
        for part in range(2):
            base = (part * 2 + sig) * ROWS * 8
            frame = [None] + [ext[pl.ds(base + r, ROWS, stride=8), :] for r in range(1, 8)]
            both.append(
                [
                    weights[0] * frame[j + 1]
                    + weights[1] * frame[j + 2]
                    + weights[2] * frame[j + 3]
                    + weights[3] * frame[j + 4]
                    for j in range(4)
                ]
            )
        for j in range(4):
            columns.append(jnp.concatenate([both[0][j], both[1][j]], axis=0))
    filt = jnp.concatenate(columns, axis=1)
    high = filt.astype(BF16)
    low = (filt - high.astype(F32)).astype(BF16)
    mid = jnp.dot(
        first[...], jnp.concatenate([high, low, high], axis=0), preferred_element_type=F32
    )
    cos, sin = twist[:ROWS, :], twist[ROWS:, :]
    turned = []
    for sj in range(8):
        real = mid[:ROWS, sj * COLS : (sj + 1) * COLS]
        imag = mid[ROWS:, sj * COLS : (sj + 1) * COLS]
        turned.append(jnp.concatenate([real * cos + imag * sin, imag * cos - real * sin], axis=1))
    turned = jnp.concatenate(turned, axis=0)
    high = turned.astype(BF16)
    low = (turned - high.astype(F32)).astype(BF16)
    out = lax.dot_general(
        second[...],
        jnp.concatenate([high, low, high], axis=1),
        (((1,), (1,)), ((), ())),
        preferred_element_type=F32,
    )
    quarter = lax.broadcasted_iota(jnp.int32, (ROWS, COLS), 1) // ROWS
    for part in range(2):
        for half in range(2):
            block = [
                out[(part * 4 + r) * 32 : (part * 4 + r + 1) * 32, half * 128 : (half + 1) * 128]
                for r in range(4)
            ]
            for b in range(4):
                moved = [
                    block[r] if r == b else pltpu.roll(block[r], 32 * ((r - b) % 4), 1)
                    for r in range(4)
                ]
                spec = jnp.where(
                    quarter < 2,
                    jnp.where(quarter == 0, moved[0], moved[1]),
                    jnp.where(quarter == 2, moved[2], moved[3]),
                )
                index = part * 8 + half * 4 + b
                by_row[index * 32 : (index + 1) * 32, :] = spec.astype(BF16)
                mixed[pl.ds(index, 32, stride=16), :] = spec
    by_tile[...] = mixed[...].astype(BF16)


def spectra(own, past):
    channels = own.shape[3]
    consts = [jnp.asarray(t) for t in tables(channels)]
    return pl.pallas_call(
        spectra_kernel,
        out_shape=[jax.ShapeDtypeStruct((512, COLS), BF16)] * 2,
        in_specs=[VMEM] * 6,
        out_specs=[VMEM] * 2,
        scratch_shapes=[pltpu.VMEM((4 * ROWS * 8, COLS), F32), pltpu.VMEM((512, COLS), F32)],
        compiler_params=pltpu.CompilerParams(vmem_limit_bytes=32 << 20),
        cost_estimate=pl.CostEstimate(flops=120_000_000, bytes_accessed=900_000, transcendentals=0),
    )(own, past, *consts)


def pick_kernel(peers, roots, pieces, out):
    for k in range(STEPS):
        piece = pieces[pl.ds(pl.multiple_of(roots[k] * 16, 16), 16), :]
        for peer in range(peers):
            out[peer * 64 + k * 16 : peer * 64 + (k + 1) * 16, :] = piece


def pick(roots, pieces, peers):
    return pl.pallas_call(
        lambda *refs: pick_kernel(peers, *refs),
        out_shape=jax.ShapeDtypeStruct((peers * 64, COLS), BF16),
        in_specs=[SMEM, VMEM],
        out_specs=VMEM,
        compiler_params=pltpu.CompilerParams(vmem_limit_bytes=32 << 20),
        cost_estimate=pl.CostEstimate(flops=0, bytes_accessed=400_000, transcendentals=0),
    )(roots, pieces)


def correlate_kernel(valid, core, own, near, far, out, mine, theirs):
    for place, block in ((core[0], near), (1 - core[0], far)):
        for peer in range(16):
            start = pl.multiple_of((2 * peer + place) * 64, 64)
            theirs[pl.ds(start, 64), :] = block[peer * 64 : (peer + 1) * 64, :].astype(F32)
    count = valid[0]
    weight = 1.0 / jnp.full((8, COLS), count, jnp.int32).astype(F32)
    nothing = jnp.zeros((8, COLS), F32)
    for j in range(4):
        scale = jnp.concatenate([jnp.where(j < count, weight, nothing)] * 4, axis=0)
        for ps in range(4):
            rows = slice((ps * 4 + j) * 32, (ps * 4 + j + 1) * 32)
            mine[rows, :] = own[rows, :].astype(F32) * scale
    for block in range(4):
        left = [
            mine[i * 32 + block * 8 : i * 32 + block * 8 + 8, :] for i in range(16)
        ]
        for k in range(STEPS):
            for q in range(2):
                start = block * 8 * 64 + k * 16 + q * 4
                real = [theirs[pl.ds(start + j, 8, stride=64), :] for j in range(4)]
                imag = [theirs[pl.ds(start + 8 + j, 8, stride=64), :] for j in range(4)]
                for s in range(2):
                    vis_real, vis_imag = nothing, nothing
                    for j in range(4):
                        a, b = left[s * 4 + j], left[8 + s * 4 + j]
                        vis_real = vis_real + (a * real[j] + b * imag[j])
                        vis_imag = vis_imag + (b * real[j] - a * imag[j])
                    at = (k * 2 + s) * 64 + block * 16 + q
                    out[pl.ds(at, 8, stride=2), :] = vis_real
                    out[pl.ds(512 + at, 8, stride=2), :] = vis_imag


def correlate(valid, core, own, near, far):
    return pl.pallas_call(
        correlate_kernel,
        out_shape=jax.ShapeDtypeStruct((1024, COLS), F32),
        in_specs=[SMEM, SMEM, VMEM, VMEM, VMEM],
        out_specs=VMEM,
        scratch_shapes=[pltpu.VMEM((512, COLS), F32), pltpu.VMEM((2048, COLS), F32)],
        compiler_params=pltpu.CompilerParams(vmem_limit_bytes=32 << 20),
        cost_estimate=pl.CostEstimate(flops=4_000_000, bytes_accessed=1_200_000, transcendentals=0),
    )(valid, core, own, near, far)


def local(samples, valid_spectra, root_blocks):
    blocks, places = lax.axis_size("tm"), lax.axis_size("stn")
    past = lax.ppermute(samples, "tm", [(b, b + 1) for b in range(blocks - 1)])
    by_tile, by_row = spectra(samples, past)
    pieces = lax.all_to_all(by_tile, "stn", 0, 0, tiled=True)
    picked = pick(root_blocks, pieces, places // 2)
    same_core = [[2 * p + c for p in range(places // 2)] for c in range(2)]
    near = lax.all_to_all(picked, "stn", 0, 0, axis_index_groups=same_core, tiled=True)
    far = lax.ppermute(near, "stn", [(d, d ^ 1) for d in range(places)])
    core = (lax.axis_index("stn") % 2).astype(jnp.int32).reshape(1)
    vis = correlate(valid_spectra, core, by_row, near, far)
    vis = vis.reshape(2, STEPS, 2, 32, 2, COLS).transpose(0, 1, 2, 4, 3, 5)
    return vis.reshape(1, 2, STEPS, 2, 2, 32 * COLS)


def solution(mesh):
    return jax.shard_map(
        local,
        mesh=mesh,
        in_specs=(P(None, "stn", "tm", None), P("tm"), P()),
        out_specs=P("tm", None, None, "stn", None, None),
        check_vma=False,
    )
```

time: 338 us -> 63.9 us (0.19)
  the two profiles are of different devices: /device:TPU:1 before, /device:TPU:257 now
where the time goes in v1:
time: 63.9 us; the launch traced here: 63.4 us
  blocking collectives  38.4 us (60%)
  waiting for transfers between devices  9.76 us (15%)
  starting transfers between devices  6.76 us (11%)
  local copies, waits for them, and re-layouts  4.91 us (8%)
  Pallas kernels  2.91 us (5%)
  between operations  0.7 us (1%)
    all_to_all x1, blocking collectives, local(): pieces = lax.all_to_all(by_tile, 'stn', 0, 0, tiled=True)  25.5 us
    all_to_all x1, blocking collectives, local(): lax.all_to_all(picked, 'stn', 0, 0, axis_index_groups=same_core, tiled=True)  12.9 us
    ppermute x1, waiting for transfers between devices, local(): past = lax.ppermute(samples, 'tm', [(b, b + 1) for b in range(blocks - 1)])  9.27 us
    unnamed x12, local copies, waits for them, and re-layouts  4.91 us
    ppermute x1, starting transfers between devices, local(): far = lax.ppermute(near, 'stn', [(d, d ^ 1) for d in range(places)])  3.57 us
    ppermute x1, starting transfers between devices, local(): past = lax.ppermute(samples, 'tm', [(b, b + 1) for b in range(blocks - 1)])  3.19 us
    pallas_call x1, Pallas kernels, correlate(): pl.pallas_call(correlate_kernel, out_shape=jax.ShapeDtypeStruct((1024, CO...  1.46 us
  transfers between devices with their start and end apart: 2, of which 2 were waited for; matrix products, arithmetic and copies ran while one was open for 0% of the time, Pallas kernels for 0%

profile of v1, /device:TPU:257, one launch (start us, length us, event | category | flops | bytes accessed | tf_op | source)
XLA Modules:
  0.0 63.4 jit_solution(15029800922916389244)
XLA Ops:
  0.0 3.2 %collective-permute-start = (bf16[2,2,4,4096]{3,2,1,0:T(4,128)(2,1)}, bf16[2,2,4,4096]{3,2,1,0:T(4,128)(2,1)S(1)}, u32[]{:S(2)}, u32[]{:S(2)}) collective-permute-start(bf16[2,2,4,4096]{3,2,1,0:T(4,128)(2,1)} %own.1), channel_id=1, source_target_pairs={{0,1},{1,2},{2,3},{3,4},{4,5},{5,6},{6,7},{7,8},{8,9},{9,10},{10,1... | collective-permute-start | bytes 393224 | tf_op jit(solution)/shard_map/ppermute | solution.py:199
  3.2 9.3 %collective-permute-done.past = bf16[2,2,4,4096]{3,2,1,0:T(4,128)(2,1)S(1)} collective-permute-done((bf16[2,2,4,4096]{3,2,1,0:T(4,128)(2,1)}, bf16[2,2,4,4096]{3,2,1,0:T(4,128)(2,1)S(1)}, u32[]{:S(2)}, u32[]{:S(2)}) %collective-permute-start) | collective-permute-done | bytes 131104 | tf_op jit(solution)/shard_map/ppermute | solution.py:199
  12.5 0.0 copy-start
  12.5 1.0 %copy-done = bf16[256,768]{1,0:T(8,128)(2,1)S(1)} copy-done((bf16[256,768]{1,0:T(8,128)(2,1)S(1)}, bf16[256,768]{1,0:T(8,128)(2,1)}, u32[]{:S(2)}) %copy-start) | copy-done | bytes 393240
  13.5 0.0 copy-start.1
  13.5 0.9 %copy-done.1 = bf16[2,2,4,4096]{3,2,1,0:T(4,128)(2,1)S(1)} copy-done((bf16[2,2,4,4096]{3,2,1,0:T(4,128)(2,1)S(1)}, bf16[2,2,4,4096]{3,2,1,0:T(4,128)(2,1)}, u32[]{:S(2)}) %copy-start.1) | copy-done | bytes 131096
  14.4 0.0 copy-start.2
  14.4 0.8 %copy-done.2 = f32[128,128]{1,0:T(8,128)S(1)} copy-done((f32[128,128]{1,0:T(8,128)S(1)}, f32[128,128]{1,0:T(8,128)}, u32[]{:S(2)}) %copy-start.2) | copy-done | bytes 65560
  15.2 0.0 copy-start.3
  15.2 0.8 %copy-done.3 = f32[64,128]{1,0:T(8,128)S(1)} copy-done((f32[64,128]{1,0:T(8,128)S(1)}, f32[64,128]{1,0:T(8,128)}, u32[]{:S(2)}) %copy-start.3) | copy-done | bytes 32792
  16.0 0.0 copy-start.4
  16.0 0.8 %copy-done.4 = bf16[64,192]{1,0:T(8,128)(2,1)S(1)} copy-done((bf16[64,192]{1,0:T(8,128)(2,1)S(1)}, bf16[64,192]{1,0:T(8,128)(2,1)}, u32[]{:S(2)}) %copy-start.4) | copy-done | bytes 24600
  16.7 0.9 %shard_map.73 = (bf16[512,128]{1,0:T(8,128)(2,1)S(1)}, bf16[512,128]{1,0:T(8,128)(2,1)S(1)}) custom-call(bf16[2,2,4,4096]{3,2,1,0:T(4,128)(2,1)S(1)} %copy-done.1, bf16[2,2,4,4096]{3,2,1,0:T(4,128)(2,1)S(1)} %collective-permute-done.past, f32[128,128]{1,0:T(8,128)S(1)} %copy-done.2, bf16[64,192]{1,0:T(8,128)(2,1)S(1)} %copy-done.4, f32[64,128]{1,0:T(8,128)S(1)} %copy-done.3, ...), custom_call_target="tpu_custom_call" | custom-call | flops 120000000 | bytes 900000 | tf_op jit(solution)/shard_map/pallas_call | solution.py:123
  17.6 25.5 %all_to_all.22 = bf16[32,16,128]{2,1,0:T(8,128)(2,1)S(1)} all-to-all(bf16[32,16,128]{2,1,0:T(8,128)(2,1)S(1)} %bitcast.14), channel_id=1, replica_groups=mesh['stn'=32,'tm'=24] {'stn'}, dimensions={0} | all-to-all | bytes 262144 | tf_op jit(solution)/shard_map/all_to_all | solution.py:201
  43.1 0.0 copy-start.5
  43.1 0.7 %copy-done.5 = s32[4]{0:T(128)S(1)} copy-done((s32[4]{0:T(128)S(1)}, s32[4]{0:T(128)}, u32[]{:S(2)}) %copy-start.5) | copy-done | bytes 40
  43.8 0.6 shard_map.74
  44.4 12.9 %all_to_all.23 = bf16[16,64,128]{2,1,0:T(8,128)(2,1)S(1)} all-to-all(bf16[16,64,128]{2,1,0:T(8,128)(2,1)S(1)} %bitcast.10), channel_id=1, replica_groups={{0,48,96,144,192,240,288,336,384,432,480,528,576,624,672,720},{24,72,12..., dimensions={0} | all-to-all | bytes 524288 | tf_op jit(solution)/shard_map/all_to_all | solution.py:204
  57.2 3.6 %collective-permute-start.1 = (bf16[1024,128]{1,0:T(8,128)(2,1)S(1)}, bf16[1024,128]{1,0:T(8,128)(2,1)S(1)}, u32[]{:S(2)}, u32[]{:S(2)}) collective-permute-start(bf16[1024,128]{1,0:T(8,128)(2,1)S(1)} %bitcast.11), channel_id=1, source_target_pairs={{0,24},{24,0},{48,72},{72,48},{96,120},{120,96},{144,168},{168,144... | collective-permute-start | bytes 786440 | tf_op jit(solution)/shard_map/ppermute | solution.py:205
  61.5 0.5 collective-permute-done.1.far
  62.0 1.5 %shard_map.75 = f32[1024,128]{1,0:T(8,128)} custom-call(s32[1]{0:T(128)S(6)} %copy.9.valid, s32[1]{0:T(128)} %bitcast.core, bf16[512,128]{1,0:T(8,128)(2,1)S(1)} %get-tuple-element.7.own, bf16[1024,128]{1,0:T(8,128)(2,1)S(1)} %bitcast.12, bf16[1024,128]{1,0:T(8,128)(2,1)S(1)} %collective-permute-done.1.far), custom_call_target="tpu_custom_call" | custom-call | flops 4000000 | bytes 1200000 | tf_op jit(solution)/shard_map/pallas_call | solution.py:186
Async XLA Ops:
  0.0 12.5 %collective-permute-start = (bf16[2,2,4,4096]{3,2,1,0:T(4,128)(2,1)}, bf16[2,2,4,4096]{3,2,1,0:T(4,128)(2,1)S(1)}, u32[]{:S(2)}, u32[]{:S(2)}) collective-permute-start(bf16[2,2,4,4096]{3,2,1,0:T(4,128)(2,1)} %own.1), channel_id=1, source_target_pairs={{0,1},{1,2},{2,3},{3,4},{4,5},{5,6},{6,7},{7,8},{8,9},{9,10},{10,1... | collective-permute-start | bytes 393224 | tf_op jit(solution)/shard_map/ppermute | solution.py:199
  12.5 1.0 %copy-start = (bf16[256,768]{1,0:T(8,128)(2,1)S(1)}, bf16[256,768]{1,0:T(8,128)(2,1)}, u32[]{:S(2)}) copy-start(bf16[256,768]{1,0:T(8,128)(2,1)} %constant.29.clone.second) | copy-start | bytes 1179652
  13.5 0.9 %copy-start.1 = (bf16[2,2,4,4096]{3,2,1,0:T(4,128)(2,1)S(1)}, bf16[2,2,4,4096]{3,2,1,0:T(4,128)(2,1)}, u32[]{:S(2)}) copy-start(bf16[2,2,4,4096]{3,2,1,0:T(4,128)(2,1)} %own.1) | copy-start | bytes 393220
  14.4 0.8 %copy-start.2 = (f32[128,128]{1,0:T(8,128)S(1)}, f32[128,128]{1,0:T(8,128)}, u32[]{:S(2)}) copy-start(f32[128,128]{1,0:T(8,128)} %constant.26.clone.taps) | copy-start | bytes 196612
  15.2 0.8 %copy-start.3 = (f32[64,128]{1,0:T(8,128)S(1)}, f32[64,128]{1,0:T(8,128)}, u32[]{:S(2)}) copy-start(f32[64,128]{1,0:T(8,128)} %constant.28.clone.twist) | copy-start | bytes 98308
  16.0 0.8 %copy-start.4 = (bf16[64,192]{1,0:T(8,128)(2,1)S(1)}, bf16[64,192]{1,0:T(8,128)(2,1)}, u32[]{:S(2)}) copy-start(bf16[64,192]{1,0:T(8,128)(2,1)} %constant.27.clone.first) | copy-start | bytes 73732
  43.1 0.7 %copy-start.5 = (s32[4]{0:T(128)S(1)}, s32[4]{0:T(128)}, u32[]{:S(2)}) copy-start(s32[4]{0:T(128)} %refs_0_.1) | copy-start | bytes 52
  57.2 4.7 %collective-permute-start.1 = (bf16[1024,128]{1,0:T(8,128)(2,1)S(1)}, bf16[1024,128]{1,0:T(8,128)(2,1)S(1)}, u32[]{:S(2)}, u32[]{:S(2)}) collective-permute-start(bf16[1024,128]{1,0:T(8,128)(2,1)S(1)} %bitcast.11), channel_id=1, source_target_pairs={{0,24},{24,0},{48,72},{72,48},{96,120},{120,96},{144,168},{168,144... | collective-permute-start | bytes 786440 | tf_op jit(solution)/shard_map/ppermute | solution.py:205

commit v2 on v1

--- a/solution.py
+++ b/solution.py
@@ -16,6 +16,7 @@
 F32, BF16 = jnp.float32, jnp.bfloat16
 VMEM = pl.BlockSpec(memory_space=pltpu.VMEM)
 SMEM = pl.BlockSpec(memory_space=pltpu.SMEM)
+HBM = pl.BlockSpec(memory_space=pltpu.HBM)
 
 
 def split(table):
@@ -45,32 +46,110 @@
     return taps, first, twist, second
 
 
-def spectra_kernel(own, past, taps, first, twist, second, by_tile, by_row, ext, mixed):
+def tails_kernel(samples, tails, rows, held, mixed, sems):
+    copies = [
+        pltpu.make_async_copy(samples.at[part, sig], held.at[part, sig], sems.at[part * 2 + sig])
+        for part in range(2)
+        for sig in range(2)
+    ]
+    for copy in copies:
+        copy.start()
     for part in range(2):
+        copies[part * 2].wait()
+        copies[part * 2 + 1].wait()
+        both = jnp.concatenate(
+            [held[part, 0].astype(F32), held[part, 1].astype(F32)], axis=0
+        )
+        for tile in range(ROWS):
+            start = (part * ROWS + tile) * 8
+            mixed[start : start + 8, :] = both[:, tile * COLS : (tile + 1) * COLS]
         for sig in range(2):
-            base = (part * 2 + sig) * ROWS * 8
-            before = past[part, sig].astype(F32)
-            now = own[part, sig].astype(F32)
-            for tile in range(ROWS):
-                lanes = slice(tile * COLS, (tile + 1) * COLS)
-                ext[base + tile * 8 : base + tile * 8 + 4, :] = before[:, lanes]
-                ext[base + tile * 8 + 4 : base + tile * 8 + 8, :] = now[:, lanes]
+            for frame in range(4):
+                row = mixed[pl.ds(part * ROWS * 8 + sig * 4 + frame, ROWS, stride=8), :]
+                index = part * 2 + sig
+                rows[(index * 4 + frame) * 32 : (index * 4 + frame + 1) * 32, :] = row
+                if frame > 0:
+                    start = (index * 3 + frame - 1) * 32
+                    tails[start : start + 32, :] = row.astype(BF16)
+
+
+def tails_of(samples):
+    return pl.pallas_call(
+        tails_kernel,
+        out_shape=[
+            jax.ShapeDtypeStruct((384, COLS), BF16),
+            jax.ShapeDtypeStruct((512, COLS), F32),
+        ],
+        in_specs=[HBM],
+        out_specs=[VMEM] * 2,
+        scratch_shapes=[
+            pltpu.VMEM(samples.shape, BF16),
+            pltpu.VMEM((512, COLS), F32),
+            pltpu.SemaphoreType.DMA((4,)),
+        ],
+        compiler_params=pltpu.CompilerParams(vmem_limit_bytes=32 << 20),
+        cost_estimate=pl.CostEstimate(flops=0, bytes_accessed=600_000, transcendentals=0),
+    )(samples)
+
+
+def ready_kernel(rows, valid, roots, taps, first, twist, second, part_sums, *rest):
+    near, numbers, sems = rest[:4], rest[4], rest[5]
+    copies = [
+        pltpu.make_async_copy(table, place, sems.at[i])
+        for i, (table, place) in enumerate(zip((taps, first, twist, second), near))
+    ]
+    for copy in copies:
+        copy.start()
+    for k in range(STEPS):
+        numbers[k] = roots[k]
+    numbers[STEPS] = valid[0]
+    numbers[STEPS + 1] = lax.rem(lax.axis_index("stn"), 2)
+    copies[0].wait()
+    weights = [near[0][k * ROWS : (k + 1) * ROWS, :] for k in range(TAPS)]
+    for index in range(4):
+        frame = [rows[(index * 4 + f) * 32 : (index * 4 + f + 1) * 32, :] for f in range(4)]
+        for j in range(4):
+            total = weights[3 - j] * frame[0]
+            for f in range(1, j + 1):
+                total = total + weights[3 - j + f] * frame[f]
+            part_sums[(index * 4 + j) * 32 : (index * 4 + j + 1) * 32, :] = total
+    for copy in copies[1:]:
+        copy.wait()
+
+
+def ready(rows, valid, roots, channels):
+    consts = [jnp.asarray(t) for t in tables(channels)]
+    return pl.pallas_call(
+        ready_kernel,
+        out_shape=[jax.ShapeDtypeStruct((512, COLS), F32)]
+        + [jax.ShapeDtypeStruct(c.shape, c.dtype) for c in consts]
+        + [jax.ShapeDtypeStruct((STEPS + 2,), jnp.int32)],
+        in_specs=[VMEM, SMEM, SMEM] + [HBM] * 4,
+        out_specs=[VMEM] * 5 + [SMEM],
+        scratch_shapes=[pltpu.SemaphoreType.DMA((4,))],
+        compiler_params=pltpu.CompilerParams(vmem_limit_bytes=32 << 20),
+        cost_estimate=pl.CostEstimate(flops=700_000, bytes_accessed=900_000, transcendentals=0),
+    )(rows, valid, roots, *consts)
+
+
+def spectra_kernel(past, part_sums, taps, first, twist, second, by_tile, by_row, mixed):
     weights = [taps[k * ROWS : (k + 1) * ROWS, :] for k in range(TAPS)]
     columns = []
     for sig in range(2):
         both = []
         for part in range(2):
-            base = (part * 2 + sig) * ROWS * 8
-            frame = [None] + [ext[pl.ds(base + r, ROWS, stride=8), :] for r in range(1, 8)]
-            both.append(
-                [
-                    weights[0] * frame[j + 1]
-                    + weights[1] * frame[j + 2]
-                    + weights[2] * frame[j + 3]
-                    + weights[3] * frame[j + 4]
-                    for j in range(4)
-                ]
-            )
+            index = part * 2 + sig
+            frame = [
+                past[(index * 3 + f) * 32 : (index * 3 + f + 1) * 32, :].astype(F32)
+                for f in range(3)
+            ]
+            sums = [
+                part_sums[(index * 4 + j) * 32 : (index * 4 + j + 1) * 32, :] for j in range(4)
+            ]
+            for j in range(3):
+                for k in range(3 - j):
+                    sums[j] = sums[j] + weights[k] * frame[j + k]
+            both.append(sums)
         for j in range(4):
             columns.append(jnp.concatenate([both[0][j], both[1][j]], axis=0))
     filt = jnp.concatenate(columns, axis=1)
@@ -117,18 +196,16 @@
     by_tile[...] = mixed[...].astype(BF16)
 
 
-def spectra(own, past):
-    channels = own.shape[3]
-    consts = [jnp.asarray(t) for t in tables(channels)]
+def spectra(past, *prepared):
     return pl.pallas_call(
         spectra_kernel,
         out_shape=[jax.ShapeDtypeStruct((512, COLS), BF16)] * 2,
         in_specs=[VMEM] * 6,
         out_specs=[VMEM] * 2,
-        scratch_shapes=[pltpu.VMEM((4 * ROWS * 8, COLS), F32), pltpu.VMEM((512, COLS), F32)],
+        scratch_shapes=[pltpu.VMEM((512, COLS), F32)],
         compiler_params=pltpu.CompilerParams(vmem_limit_bytes=32 << 20),
         cost_estimate=pl.CostEstimate(flops=120_000_000, bytes_accessed=900_000, transcendentals=0),
-    )(own, past, *consts)
+    )(past, *prepared)
 
 
 def pick_kernel(peers, roots, pieces, out):
@@ -149,12 +226,13 @@
     )(roots, pieces)
 
 
-def correlate_kernel(valid, core, own, near, far, out, mine, theirs):
-    for place, block in ((core[0], near), (1 - core[0], far)):
+def correlate_kernel(numbers, own, near, far, out, mine, theirs):
+    core = numbers[STEPS + 1]
+    for place, block in ((core, near), (1 - core, far)):
         for peer in range(16):
             start = pl.multiple_of((2 * peer + place) * 64, 64)
             theirs[pl.ds(start, 64), :] = block[peer * 64 : (peer + 1) * 64, :].astype(F32)
-    count = valid[0]
+    count = numbers[STEPS]
     weight = 1.0 / jnp.full((8, COLS), count, jnp.int32).astype(F32)
     nothing = jnp.zeros((8, COLS), F32)
     for j in range(4):
@@ -182,29 +260,30 @@
                     out[pl.ds(512 + at, 8, stride=2), :] = vis_imag
 
 
-def correlate(valid, core, own, near, far):
+def correlate(numbers, own, near, far):
     return pl.pallas_call(
         correlate_kernel,
         out_shape=jax.ShapeDtypeStruct((1024, COLS), F32),
-        in_specs=[SMEM, SMEM, VMEM, VMEM, VMEM],
+        in_specs=[SMEM, VMEM, VMEM, VMEM],
         out_specs=VMEM,
         scratch_shapes=[pltpu.VMEM((512, COLS), F32), pltpu.VMEM((2048, COLS), F32)],
         compiler_params=pltpu.CompilerParams(vmem_limit_bytes=32 << 20),
         cost_estimate=pl.CostEstimate(flops=4_000_000, bytes_accessed=1_200_000, transcendentals=0),
-    )(valid, core, own, near, far)
+    )(numbers, own, near, far)
 
 
 def local(samples, valid_spectra, root_blocks):
     blocks, places = lax.axis_size("tm"), lax.axis_size("stn")
-    past = lax.ppermute(samples, "tm", [(b, b + 1) for b in range(blocks - 1)])
-    by_tile, by_row = spectra(samples, past)
+    tails, rows = tails_of(samples)
+    past = lax.ppermute(tails, "tm", [(b, b + 1) for b in range(blocks - 1)])
+    *prepared, numbers = ready(rows, valid_spectra, root_blocks, samples.shape[3])
+    by_tile, by_row = spectra(past, *prepared)
     pieces = lax.all_to_all(by_tile, "stn", 0, 0, tiled=True)
-    picked = pick(root_blocks, pieces, places // 2)
+    picked = pick(numbers, pieces, places // 2)
     same_core = [[2 * p + c for p in range(places // 2)] for c in range(2)]
     near = lax.all_to_all(picked, "stn", 0, 0, axis_index_groups=same_core, tiled=True)
     far = lax.ppermute(near, "stn", [(d, d ^ 1) for d in range(places)])
-    core = (lax.axis_index("stn") % 2).astype(jnp.int32).reshape(1)
-    vis = correlate(valid_spectra, core, by_row, near, far)
+    vis = correlate(numbers, by_row, near, far)
     vis = vis.reshape(2, STEPS, 2, 32, 2, COLS).transpose(0, 1, 2, 4, 3, 5)
     return vis.reshape(1, 2, STEPS, 2, 2, 32 * COLS)
 

time: 63.9 us -> 57.6 us (0.901)
  waiting for transfers between devices: 9.76 us -> 5.42 us
  local copies, waits for them, and re-layouts: 4.91 us -> 2.53 us
  Pallas kernels: 2.91 us -> 5.23 us
  blocking collectives: 38.4 us -> 36.6 us
    ppermute x1, waiting for transfers between devices: 9.27 us -> 4.28 us  [local(): past = lax.ppermute(tails, 'tm', [(b, b + 1) for b in range(blocks - 1)])]
    unnamed x12, local copies, waits for them, and re-layouts: 4.91 us -> 2.53 us
    pallas_call x0 -> x2, Pallas kernels: none -> 1.88 us  [the longest x1 1.59 us: ready(): pl.pallas_call(ready_kernel, out_shape=[jax.ShapeDtypeStruct((512, COLS),...]
    all_to_all x1, blocking collectives: 25.5 us -> 23.7 us  [local(): pieces = lax.all_to_all(by_tile, 'stn', 0, 0, tiled=True)]
    ppermute x1, waiting for transfers between devices: 0.48 us -> 1.14 us  [local(): far = lax.ppermute(near, 'stn', [(d, d ^ 1) for d in range(places)])]
  transfers between devices with their start and end apart: 2 -> 2, of which waited for: 2 -> 2; matrix products, arithmetic and copies ran while one was open for 0% -> 0% of each run, Pallas kernels for 0% -> 3%
where the time goes in v2:
time: 57.6 us; the launch traced here: 57.3 us
  blocking collectives  36.6 us (64%)
  starting transfers between devices  6.77 us (12%)
  waiting for transfers between devices  5.42 us (9%)
  Pallas kernels  5.23 us (9%)
  local copies, waits for them, and re-layouts  2.53 us (4%)
  between operations  0.73 us (1%)
    all_to_all x1, blocking collectives, local(): pieces = lax.all_to_all(by_tile, 'stn', 0, 0, tiled=True)  23.7 us
    all_to_all x1, blocking collectives, local(): lax.all_to_all(picked, 'stn', 0, 0, axis_index_groups=same_core, tiled=True)  12.9 us
    ppermute x1, waiting for transfers between devices, local(): past = lax.ppermute(tails, 'tm', [(b, b + 1) for b in range(blocks - 1)])  4.28 us
    ppermute x1, starting transfers between devices, local(): far = lax.ppermute(near, 'stn', [(d, d ^ 1) for d in range(places)])  3.57 us
    ppermute x1, starting transfers between devices, local(): past = lax.ppermute(tails, 'tm', [(b, b + 1) for b in range(blocks - 1)])  3.2 us
    unnamed x12, local copies, waits for them, and re-layouts  2.53 us
    pallas_call x1, Pallas kernels, correlate(): pl.pallas_call(correlate_kernel, out_shape=jax.ShapeDtypeStruct((1024, CO...  2 us
    pallas_call x1, Pallas kernels, ready(): pl.pallas_call(ready_kernel, out_shape=[jax.ShapeDtypeStruct((512, COLS),...  1.59 us
  transfers between devices with their start and end apart: 2, of which 2 were waited for; matrix products, arithmetic and copies ran while one was open for 0% of the time, Pallas kernels for 3%

profile of v2, /device:TPU:257, one launch (start us, length us, event | category | flops | bytes accessed | tf_op | source)
XLA Modules:
  0.0 57.3 jit_solution(4845742756592767192)
XLA Ops:
  0.0 0.0 copy-start.1
  0.0 0.9 %copy-done.1 = bf16[2,2,4,4096]{3,2,1,0:T(4,128)(2,1)S(1)} copy-done((bf16[2,2,4,4096]{3,2,1,0:T(4,128)(2,1)S(1)}, bf16[2,2,4,4096]{3,2,1,0:T(4,128)(2,1)}, u32[]{:S(2)}) %copy-start.1) | copy-done | bytes 131096
  0.9 0.0 copy-start.2
  0.9 0.0 copy-start.3
  0.9 0.0 copy-start.4
  0.9 0.3 shard_map.73
  1.2 3.2 %collective-permute-start = (bf16[384,128]{1,0:T(8,128)(2,1)S(1)}, bf16[384,128]{1,0:T(8,128)(2,1)S(1)}, u32[]{:S(2)}, u32[]{:S(2)}) collective-permute-start(bf16[384,128]{1,0:T(8,128)(2,1)S(1)} %get-tuple-element.17), channel_id=1, source_target_pairs={{0,1},{1,2},{2,3},{3,4},{4,5},{5,6},{6,7},{7,8},{8,9},{9,10},{10,1... | collective-permute-start | bytes 294920 | tf_op jit(solution)/shard_map/ppermute | solution.py:278
  5.1 0.0 copy-start.5
  5.1 0.0 copy-done.2
  5.1 0.0 copy-done.3
  5.1 0.0 copy-done.4
  5.1 0.6 %copy-done.5 = s32[4]{0:T(128)S(1)} copy-done((s32[4]{0:T(128)S(1)}, s32[4]{0:T(128)}, u32[]{:S(2)}) %copy-start.5) | copy-done | bytes 40
  5.7 0.0 copy-start
  5.7 1.0 %copy-done = bf16[256,768]{1,0:T(8,128)(2,1)S(1)} copy-done((bf16[256,768]{1,0:T(8,128)(2,1)S(1)}, bf16[256,768]{1,0:T(8,128)(2,1)}, u32[]{:S(2)}) %copy-start) | copy-done | bytes 393240
  6.7 1.6 %shard_map.74 = (f32[512,128]{1,0:T(8,128)S(1)}, f32[128,128]{1,0:T(8,128)S(1)}, bf16[64,192]{1,0:T(8,128)(2,1)S(1)}, f32[64,128]{1,0:T(8,128)S(1)}, bf16[256,768]{1,0:T(8,128)(2,1)S(1)}, /*index=5*/s32[6]{0:T(128)S(1)}) custom-call(f32[512,128]{1,0:T(8,128)S(1)} %get-tuple-element.15.rows, s32[1]{0:T(128)S(6)} %copy.9.valid, s32[4]{0:T(128)S(1)} %copy-done.5, ...), custom_call_target="tpu_custom_call" | custom-call | flops 700000 | bytes 900000 | tf_op jit(solution)/shard_map/pallas_call | solution.py:122
  8.3 4.3 %collective-permute-done.past = bf16[384,128]{1,0:T(8,128)(2,1)S(1)} collective-permute-done((bf16[384,128]{1,0:T(8,128)(2,1)S(1)}, bf16[384,128]{1,0:T(8,128)(2,1)S(1)}, u32[]{:S(2)}, u32[]{:S(2)}) %collective-permute-start) | collective-permute-done | bytes 98336 | tf_op jit(solution)/shard_map/ppermute | solution.py:278
  12.6 0.8 %shard_map.75 = (bf16[512,128]{1,0:T(8,128)(2,1)S(1)}, bf16[512,128]{1,0:T(8,128)(2,1)S(1)}) custom-call(bf16[384,128]{1,0:T(8,128)(2,1)S(1)} %collective-permute-done.past, f32[512,128]{1,0:T(8,128)S(1)} %get-tuple-element.18.part_sums, f32[128,128]{1,0:T(8,128)S(1)} %get-tuple-element.19.taps, bf16[64,192]{1,0:T(8,128)(2,1)S(1)} %get-tuple-element.20.first, ...), custom_call_target="tpu_custom_call" | custom-call | flops 120000000 | bytes 900000 | tf_op jit(solution)/shard_map/pallas_call | solution.py:200
  13.4 23.7 %all_to_all.22 = bf16[32,16,128]{2,1,0:T(8,128)(2,1)S(1)} all-to-all(bf16[32,16,128]{2,1,0:T(8,128)(2,1)S(1)} %bitcast.13), channel_id=1, replica_groups=mesh['stn'=32,'tm'=24] {'stn'}, dimensions={0} | all-to-all | bytes 262144 | tf_op jit(solution)/shard_map/all_to_all | solution.py:281
  37.1 0.6 %shard_map.76 = bf16[1024,128]{1,0:T(8,128)(2,1)S(1)} custom-call(s32[6]{0:T(128)S(1)} %get-tuple-element.16.refs_0_.numbers, bf16[512,128]{1,0:T(8,128)(2,1)S(1)} %bitcast.12), custom_call_target="tpu_custom_call" | custom-call | bytes 400000 | tf_op jit(solution)/shard_map/pallas_call | solution.py:219
  37.7 12.9 %all_to_all.23 = bf16[16,64,128]{2,1,0:T(8,128)(2,1)S(1)} all-to-all(bf16[16,64,128]{2,1,0:T(8,128)(2,1)S(1)} %bitcast.9), channel_id=1, replica_groups={{0,48,96,144,192,240,288,336,384,432,480,528,576,624,672,720},{24,72,12..., dimensions={0} | all-to-all | bytes 524288 | tf_op jit(solution)/shard_map/all_to_all | solution.py:284
  50.6 3.6 %collective-permute-start.1 = (bf16[1024,128]{1,0:T(8,128)(2,1)S(1)}, bf16[1024,128]{1,0:T(8,128)(2,1)S(1)}, u32[]{:S(2)}, u32[]{:S(2)}) collective-permute-start(bf16[1024,128]{1,0:T(8,128)(2,1)S(1)} %bitcast.10), channel_id=1, source_target_pairs={{0,24},{24,0},{48,72},{72,48},{96,120},{120,96},{144,168},{168,144... | collective-permute-start | bytes 786440 | tf_op jit(solution)/shard_map/ppermute | solution.py:285
  54.1 1.1 %collective-permute-done.1.far = bf16[1024,128]{1,0:T(8,128)(2,1)S(1)} collective-permute-done((bf16[1024,128]{1,0:T(8,128)(2,1)S(1)}, bf16[1024,128]{1,0:T(8,128)(2,1)S(1)}, u32[]{:S(2)}, u32[]{:S(2)}) %collective-permute-start.1) | collective-permute-done | bytes 262176 | tf_op jit(solution)/shard_map/ppermute | solution.py:285
  55.3 2.0 %shard_map.77 = f32[1024,128]{1,0:T(8,128)} custom-call(s32[6]{0:T(128)S(1)} %get-tuple-element.16.refs_0_.numbers, bf16[512,128]{1,0:T(8,128)(2,1)S(1)} %get-tuple-element.23.own, bf16[1024,128]{1,0:T(8,128)(2,1)S(1)} %bitcast.11, bf16[1024,128]{1,0:T(8,128)(2,1)S(1)} %collective-permute-done.1.far), custom_call_target="tpu_custom_call" | custom-call | flops 4000000 | bytes 1200000 | tf_op jit(solution)/shard_map/pallas_call | solution.py:264
Async XLA Ops:
  0.0 0.9 %copy-start.1 = (bf16[2,2,4,4096]{3,2,1,0:T(4,128)(2,1)S(1)}, bf16[2,2,4,4096]{3,2,1,0:T(4,128)(2,1)}, u32[]{:S(2)}) copy-start(bf16[2,2,4,4096]{3,2,1,0:T(4,128)(2,1)} %samples.1) | copy-start | bytes 393220
  0.9 4.2 %copy-start.2 = (f32[128,128]{1,0:T(8,128)S(1)}, f32[128,128]{1,0:T(8,128)}, u32[]{:S(2)}) copy-start(f32[128,128]{1,0:T(8,128)} %constant.8.clone.taps) | copy-start | bytes 196612
  0.9 4.2 %copy-start.3 = (f32[64,128]{1,0:T(8,128)S(1)}, f32[64,128]{1,0:T(8,128)}, u32[]{:S(2)}) copy-start(f32[64,128]{1,0:T(8,128)} %constant.10.clone.twist) | copy-start | bytes 98308
  0.9 4.2 %copy-start.4 = (bf16[64,192]{1,0:T(8,128)(2,1)S(1)}, bf16[64,192]{1,0:T(8,128)(2,1)}, u32[]{:S(2)}) copy-start(bf16[64,192]{1,0:T(8,128)(2,1)} %constant.9.clone.first) | copy-start | bytes 73732
  1.2 11.4 %collective-permute-start = (bf16[384,128]{1,0:T(8,128)(2,1)S(1)}, bf16[384,128]{1,0:T(8,128)(2,1)S(1)}, u32[]{:S(2)}, u32[]{:S(2)}) collective-permute-start(bf16[384,128]{1,0:T(8,128)(2,1)S(1)} %get-tuple-element.17), channel_id=1, source_target_pairs={{0,1},{1,2},{2,3},{3,4},{4,5},{5,6},{6,7},{7,8},{8,9},{9,10},{10,1... | collective-permute-start | bytes 294920 | tf_op jit(solution)/shard_map/ppermute | solution.py:278
  5.1 0.7 %copy-start.5 = (s32[4]{0:T(128)S(1)}, s32[4]{0:T(128)}, u32[]{:S(2)}) copy-start(s32[4]{0:T(128)} %roots.1) | copy-start | bytes 52
  5.7 1.0 %copy-start = (bf16[256,768]{1,0:T(8,128)(2,1)S(1)}, bf16[256,768]{1,0:T(8,128)(2,1)}, u32[]{:S(2)}) copy-start(bf16[256,768]{1,0:T(8,128)(2,1)} %constant.11.clone.second) | copy-start | bytes 1179652
  50.6 4.7 %collective-permute-start.1 = (bf16[1024,128]{1,0:T(8,128)(2,1)S(1)}, bf16[1024,128]{1,0:T(8,128)(2,1)S(1)}, u32[]{:S(2)}, u32[]{:S(2)}) collective-permute-start(bf16[1024,128]{1,0:T(8,128)(2,1)S(1)} %bitcast.10), channel_id=1, source_target_pairs={{0,24},{24,0},{48,72},{72,48},{96,120},{120,96},{144,168},{168,144... | collective-permute-start | bytes 786440 | tf_op jit(solution)/shard_map/ppermute | solution.py:285

commit v3 on v2

--- a/solution.py
+++ b/solution.py
@@ -73,6 +73,10 @@
                     tails[start : start + 32, :] = row.astype(BF16)
 
 
+def far_off(x):
+    return pltpu.with_memory_space_constraint(x, pltpu.HBM)
+
+
 def tails_of(samples):
     return pl.pallas_call(
         tails_kernel,
@@ -89,7 +93,7 @@
         ],
         compiler_params=pltpu.CompilerParams(vmem_limit_bytes=32 << 20),
         cost_estimate=pl.CostEstimate(flops=0, bytes_accessed=600_000, transcendentals=0),
-    )(samples)
+    )(far_off(samples))
 
 
 def ready_kernel(rows, valid, roots, taps, first, twist, second, part_sums, *rest):
@@ -123,13 +127,13 @@
         ready_kernel,
         out_shape=[jax.ShapeDtypeStruct((512, COLS), F32)]
         + [jax.ShapeDtypeStruct(c.shape, c.dtype) for c in consts]
-        + [jax.ShapeDtypeStruct((STEPS + 2,), jnp.int32)],
+        + [pltpu.SMEM((STEPS + 2,), jnp.int32)],
         in_specs=[VMEM, SMEM, SMEM] + [HBM] * 4,
         out_specs=[VMEM] * 5 + [SMEM],
         scratch_shapes=[pltpu.SemaphoreType.DMA((4,))],
         compiler_params=pltpu.CompilerParams(vmem_limit_bytes=32 << 20),
         cost_estimate=pl.CostEstimate(flops=700_000, bytes_accessed=900_000, transcendentals=0),
-    )(rows, valid, roots, *consts)
+    )(rows, valid, roots, *map(far_off, consts))
 
 
 def spectra_kernel(past, part_sums, taps, first, twist, second, by_tile, by_row, mixed):

time: 57.6 us -> 56.2 us (0.976)
  local copies, waits for them, and re-layouts: 2.53 us -> 0.65 us
  waiting for transfers between devices: 5.42 us -> 6.35 us
    unnamed x12 -> x2, local copies, waits for them, and re-layouts: 2.53 us -> 0.65 us
    ppermute x1, waiting for transfers between devices: 4.28 us -> 5.21 us  [local(): past = lax.ppermute(tails, 'tm', [(b, b + 1) for b in range(blocks - 1)])]
    pallas_call x1, Pallas kernels: 0.29 us -> 0.9 us  [tails_of(): pl.pallas_call(tails_kernel, out_shape=[jax.ShapeDtypeStruct((384, COLS),...]
where the time goes in v3:
time: 56.2 us; the launch traced here: 55.9 us
  blocking collectives  36.6 us (65%)
  starting transfers between devices  6.77 us (12%)
  waiting for transfers between devices  6.35 us (11%)
  Pallas kernels  4.81 us (9%)
  between operations  0.71 us (1%)
  local copies, waits for them, and re-layouts  0.65 us (1%)
    all_to_all x1, blocking collectives, local(): pieces = lax.all_to_all(by_tile, 'stn', 0, 0, tiled=True)  23.7 us
    all_to_all x1, blocking collectives, local(): lax.all_to_all(picked, 'stn', 0, 0, axis_index_groups=same_core, tiled=True)  12.9 us
    ppermute x1, waiting for transfers between devices, local(): past = lax.ppermute(tails, 'tm', [(b, b + 1) for b in range(blocks - 1)])  5.21 us
    ppermute x1, starting transfers between devices, local(): far = lax.ppermute(near, 'stn', [(d, d ^ 1) for d in range(places)])  3.57 us
    ppermute x1, starting transfers between devices, local(): past = lax.ppermute(tails, 'tm', [(b, b + 1) for b in range(blocks - 1)])  3.2 us
    pallas_call x1, Pallas kernels, ready(): pl.pallas_call(ready_kernel, out_shape=[jax.ShapeDtypeStruct((512, COLS),...  1.65 us
    pallas_call x1, Pallas kernels, correlate(): pl.pallas_call(correlate_kernel, out_shape=jax.ShapeDtypeStruct((1024, CO...  1.46 us
    ppermute x1, waiting for transfers between devices, local(): far = lax.ppermute(near, 'stn', [(d, d ^ 1) for d in range(places)])  1.14 us
  transfers between devices with their start and end apart: 2, of which 2 were waited for; matrix products, arithmetic and copies ran while one was open for 0% of the time, Pallas kernels for 3%

profile of v3, /device:TPU:257, one launch (start us, length us, event | category | flops | bytes accessed | tf_op | source)
XLA Modules:
  0.0 55.9 jit_solution(1733512546223001322)
XLA Ops:
  0.0 0.9 %shard_map.73 = (bf16[384,128]{1,0:T(8,128)(2,1)S(1)}, f32[512,128]{1,0:T(8,128)S(1)}) custom-call(bf16[2,2,4,4096]{3,2,1,0:T(4,128)(2,1)} %samples.1), custom_call_target="tpu_custom_call" | custom-call | bytes 600000 | tf_op jit(solution)/shard_map/pallas_call | solution.py:81
  0.9 3.2 %collective-permute-start = (bf16[384,128]{1,0:T(8,128)(2,1)S(1)}, bf16[384,128]{1,0:T(8,128)(2,1)S(1)}, u32[]{:S(2)}, u32[]{:S(2)}) collective-permute-start(bf16[384,128]{1,0:T(8,128)(2,1)S(1)} %get-tuple-element.17), channel_id=1, source_target_pairs={{0,1},{1,2},{2,3},{3,4},{4,5},{5,6},{6,7},{7,8},{8,9},{9,10},{10,1... | collective-permute-start | bytes 294920 | tf_op jit(solution)/shard_map/ppermute | solution.py:282
  4.8 0.0 copy-start
  4.8 0.6 %copy-done = s32[4]{0:T(128)S(1)} copy-done((s32[4]{0:T(128)S(1)}, s32[4]{0:T(128)}, u32[]{:S(2)}) %copy-start) | copy-done | bytes 40
  5.4 1.6 %shard_map.74 = (f32[512,128]{1,0:T(8,128)S(1)}, f32[128,128]{1,0:T(8,128)S(1)}, bf16[64,192]{1,0:T(8,128)(2,1)S(1)}, f32[64,128]{1,0:T(8,128)S(1)}, bf16[256,768]{1,0:T(8,128)(2,1)S(1)}, /*index=5*/s32[6]{0:T(128)S(4)}) custom-call(f32[512,128]{1,0:T(8,128)S(1)} %get-tuple-element.15.rows, s32[1]{0:T(128)S(6)} %copy.9.valid, s32[4]{0:T(128)S(1)} %copy-done, ...), custom_call_target="tpu_custom_call" | custom-call | flops 700000 | bytes 900000 | tf_op jit(solution)/shard_map/pallas_call | solution.py:126
  7.1 5.2 %collective-permute-done.past = bf16[384,128]{1,0:T(8,128)(2,1)S(1)} collective-permute-done((bf16[384,128]{1,0:T(8,128)(2,1)S(1)}, bf16[384,128]{1,0:T(8,128)(2,1)S(1)}, u32[]{:S(2)}, u32[]{:S(2)}) %collective-permute-start) | collective-permute-done | bytes 98336 | tf_op jit(solution)/shard_map/ppermute | solution.py:282
  12.3 0.8 %shard_map.75 = (bf16[512,128]{1,0:T(8,128)(2,1)S(1)}, bf16[512,128]{1,0:T(8,128)(2,1)S(1)}) custom-call(bf16[384,128]{1,0:T(8,128)(2,1)S(1)} %collective-permute-done.past, f32[512,128]{1,0:T(8,128)S(1)} %get-tuple-element.18.part_sums, f32[128,128]{1,0:T(8,128)S(1)} %get-tuple-element.19.taps, bf16[64,192]{1,0:T(8,128)(2,1)S(1)} %get-tuple-element.20.first, ...), custom_call_target="tpu_custom_call" | custom-call | flops 120000000 | bytes 900000 | tf_op jit(solution)/shard_map/pallas_call | solution.py:204
  13.1 23.7 %all_to_all.22 = bf16[32,16,128]{2,1,0:T(8,128)(2,1)S(1)} all-to-all(bf16[32,16,128]{2,1,0:T(8,128)(2,1)S(1)} %bitcast.13), channel_id=1, replica_groups=mesh['stn'=32,'tm'=24] {'stn'}, dimensions={0} | all-to-all | bytes 262144 | tf_op jit(solution)/shard_map/all_to_all | solution.py:285
  36.8 12.9 %all_to_all.23 = bf16[16,64,128]{2,1,0:T(8,128)(2,1)S(1)} all-to-all(bf16[16,64,128]{2,1,0:T(8,128)(2,1)S(1)} %bitcast.9), channel_id=1, replica_groups={{0,48,96,144,192,240,288,336,384,432,480,528,576,624,672,720},{24,72,12..., dimensions={0} | all-to-all | bytes 524288 | tf_op jit(solution)/shard_map/all_to_all | solution.py:288
  49.7 3.6 %collective-permute-start.1 = (bf16[1024,128]{1,0:T(8,128)(2,1)S(1)}, bf16[1024,128]{1,0:T(8,128)(2,1)S(1)}, u32[]{:S(2)}, u32[]{:S(2)}) collective-permute-start(bf16[1024,128]{1,0:T(8,128)(2,1)S(1)} %bitcast.10), channel_id=1, source_target_pairs={{0,24},{24,0},{48,72},{72,48},{96,120},{120,96},{144,168},{168,144... | collective-permute-start | bytes 786440 | tf_op jit(solution)/shard_map/ppermute | solution.py:289
  53.3 1.1 %collective-permute-done.1.far = bf16[1024,128]{1,0:T(8,128)(2,1)S(1)} collective-permute-done((bf16[1024,128]{1,0:T(8,128)(2,1)S(1)}, bf16[1024,128]{1,0:T(8,128)(2,1)S(1)}, u32[]{:S(2)}, u32[]{:S(2)}) %collective-permute-start.1) | collective-permute-done | bytes 262176 | tf_op jit(solution)/shard_map/ppermute | solution.py:289
  54.4 1.5 %shard_map.77 = f32[1024,128]{1,0:T(8,128)} custom-call(s32[6]{0:T(128)S(4)} %get-tuple-element.16.refs_0_.numbers, bf16[512,128]{1,0:T(8,128)(2,1)S(1)} %get-tuple-element.23.own, bf16[1024,128]{1,0:T(8,128)(2,1)S(1)} %bitcast.11, bf16[1024,128]{1,0:T(8,128)(2,1)S(1)} %collective-permute-done.1.far), custom_call_target="tpu_custom_call" | custom-call | flops 4000000 | bytes 1200000 | tf_op jit(solution)/shard_map/pallas_call | solution.py:268
  (1 shorter events, 0.0 us)
Async XLA Ops:
  0.9 11.4 %collective-permute-start = (bf16[384,128]{1,0:T(8,128)(2,1)S(1)}, bf16[384,128]{1,0:T(8,128)(2,1)S(1)}, u32[]{:S(2)}, u32[]{:S(2)}) collective-permute-start(bf16[384,128]{1,0:T(8,128)(2,1)S(1)} %get-tuple-element.17), channel_id=1, source_target_pairs={{0,1},{1,2},{2,3},{3,4},{4,5},{5,6},{6,7},{7,8},{8,9},{9,10},{10,1... | collective-permute-start | bytes 294920 | tf_op jit(solution)/shard_map/ppermute | solution.py:282
  4.8 0.7 %copy-start = (s32[4]{0:T(128)S(1)}, s32[4]{0:T(128)}, u32[]{:S(2)}) copy-start(s32[4]{0:T(128)} %roots.1) | copy-start | bytes 52
  49.7 4.7 %collective-permute-start.1 = (bf16[1024,128]{1,0:T(8,128)(2,1)S(1)}, bf16[1024,128]{1,0:T(8,128)(2,1)S(1)}, u32[]{:S(2)}, u32[]{:S(2)}) collective-permute-start(bf16[1024,128]{1,0:T(8,128)(2,1)S(1)} %bitcast.10), channel_id=1, source_target_pairs={{0,24},{24,0},{48,72},{72,48},{96,120},{120,96},{144,168},{168,144... | collective-permute-start | bytes 786440 | tf_op jit(solution)/shard_map/ppermute | solution.py:289

commit v4 on v1

v4 whole, which is shorter than its diff:
```python
import math

import jax
import jax.numpy as jnp
import ml_dtypes
import numpy as np
from jax import lax
from jax.experimental import pallas as pl
from jax.experimental.pallas import tpu as pltpu
from jax.sharding import PartitionSpec as P

TAPS = 4
STEPS = 4
ROWS = 32
COLS = 128
F32, BF16 = jnp.float32, jnp.bfloat16
VMEM = pl.BlockSpec(memory_space=pltpu.VMEM)
SMEM = pl.BlockSpec(memory_space=pltpu.SMEM)
HBM = pl.BlockSpec(memory_space=pltpu.HBM)


def split(table):
    high = table.astype(ml_dtypes.bfloat16)
    low = (table - high.astype(np.float64)).astype(ml_dtypes.bfloat16)
    return high, low


def tables(channels):
    position = np.arange(TAPS * channels, dtype=np.float64)
    middle = (position - 0.5 * TAPS * channels + 0.5) / channels
    window = 0.5 - 0.5 * np.cos(2.0 * np.pi * (position + 0.5) / (TAPS * channels))
    taps = (np.sinc(middle) * window).astype(np.float32).reshape(TAPS * ROWS, COLS)
    row, col = np.arange(ROWS), np.arange(COLS)
    angle = 2.0 * np.pi * (row[:, None] * row[None, :] % ROWS) / ROWS
    cos, sin = np.cos(angle), np.sin(angle)
    high, low = split(np.block([[cos, sin], [-sin, cos]]))
    first = np.concatenate([high, high, low], axis=1)
    angle = 2.0 * np.pi * (row[:, None] * col[None, :]) / channels
    twist = np.concatenate([np.cos(angle), np.sin(angle)]).astype(np.float32)
    out_col = (4 * np.arange(32)[None, :] + np.arange(4)[:, None]).reshape(-1)
    angle = 2.0 * np.pi * (out_col[:, None] * col[None, :] % COLS) / COLS
    scale = 1.0 / math.sqrt(channels)
    cos, sin = np.cos(angle) * scale, np.sin(angle) * scale
    high, low = split(np.block([[cos, sin], [-sin, cos]]))
    second = np.concatenate([high, high, low], axis=1)
    return taps, first, twist, second


def near_copies(samples, held, sems, first):
    return [
        pltpu.make_async_copy(samples.at[part, sig], held.at[part, sig], sems.at[first + part * 2 + sig])
        for part in range(2)
        for sig in range(2)
    ]


def laid_out(part, held, mixed):
    both = jnp.concatenate([held[part, 0].astype(F32), held[part, 1].astype(F32)], axis=0)
    for tile in range(ROWS):
        start = (part * ROWS + tile) * 8
        mixed[start : start + 8, :] = both[:, tile * COLS : (tile + 1) * COLS]


def frame_of(part, sig, frame, mixed):
    return mixed[pl.ds(part * ROWS * 8 + sig * 4 + frame, ROWS, stride=8), :]


def tiles_kernel(samples, roots, by_tile, numbers, held, mixed, blocks, sems):
    copies = near_copies(samples, held, sems, 0)
    scalars = pltpu.make_async_copy(roots, blocks, sems.at[4])
    for copy in copies + [scalars]:
        copy.start()
    for part in range(2):
        copies[part * 2].wait()
        copies[part * 2 + 1].wait()
        both = jnp.concatenate([held[part, 0].astype(F32), held[part, 1].astype(F32)], axis=0)
        for tile in range(ROWS):
            start = tile * 16 + part * 8
            mixed[start : start + 8, :] = both[:, tile * COLS : (tile + 1) * COLS]
    by_tile[...] = mixed[...].astype(BF16)
    scalars.wait()
    for k in range(STEPS):
        numbers[k] = blocks[k]
    numbers[STEPS] = lax.axis_index("stn")


def far_off(x):
    return pltpu.with_memory_space_constraint(x, pltpu.HBM)


def tiles_of(samples, roots):
    return pl.pallas_call(
        tiles_kernel,
        out_shape=[
            jax.ShapeDtypeStruct((512, COLS), BF16),
            pltpu.SMEM((STEPS + 1,), jnp.int32),
        ],
        in_specs=[HBM] * 2,
        out_specs=[VMEM, SMEM],
        scratch_shapes=[
            pltpu.VMEM(samples.shape, BF16),
            pltpu.VMEM((512, COLS), F32),
            pltpu.SMEM((STEPS,), jnp.int32),
            pltpu.SemaphoreType.DMA((5,)),
        ],
        compiler_params=pltpu.CompilerParams(vmem_limit_bytes=32 << 20),
        cost_estimate=pl.CostEstimate(flops=0, bytes_accessed=600_000, transcendentals=0),
    )(far_off(samples), far_off(roots))


def ready_kernel(samples, valid, after, taps, first, twist, second, part_sums, tails, *rest):
    near, numbers, held, mixed, sems = rest[:4], *rest[4:]
    tables_in = [
        pltpu.make_async_copy(table, place, sems.at[i])
        for i, (table, place) in enumerate(zip((taps, first, twist, second), near))
    ]
    own_in = near_copies(samples, held, sems, 4)
    for copy in own_in + tables_in:
        copy.start()
    tables_in[0].wait()
    weights = [near[0][k * ROWS : (k + 1) * ROWS, :] for k in range(TAPS)]
    for part in range(2):
        own_in[part * 2].wait()
        own_in[part * 2 + 1].wait()
        laid_out(part, held, mixed)
        for sig in range(2):
            index = part * 2 + sig
            frame = [frame_of(part, sig, f, mixed) for f in range(4)]
            for f in range(1, 4):
                start = (index * 3 + f - 1) * 32
                tails[start : start + 32, :] = frame[f].astype(BF16)
            for j in range(4):
                total = weights[3 - j] * frame[0]
                for f in range(1, j + 1):
                    total = total + weights[3 - j + f] * frame[f]
                part_sums[(index * 4 + j) * 32 : (index * 4 + j + 1) * 32, :] = total
    for copy in tables_in[1:]:
        copy.wait()
    numbers[0] = valid[0]
    numbers[1] = lax.axis_index("stn")


def ready(samples, valid, after):
    consts = [jnp.asarray(t) for t in tables(samples.shape[3])]
    return pl.pallas_call(
        ready_kernel,
        out_shape=[
            jax.ShapeDtypeStruct((512, COLS), F32),
            jax.ShapeDtypeStruct((384, COLS), BF16),
        ]
        + [jax.ShapeDtypeStruct(c.shape, c.dtype) for c in consts]
        + [pltpu.SMEM((2,), jnp.int32)],
        in_specs=[HBM, SMEM, VMEM] + [HBM] * 4,
        out_specs=[VMEM] * 6 + [SMEM],
        scratch_shapes=[
            pltpu.VMEM(samples.shape, BF16),
            pltpu.VMEM((512, COLS), F32),
            pltpu.SemaphoreType.DMA((8,)),
        ],
        compiler_params=pltpu.CompilerParams(vmem_limit_bytes=32 << 20),
        cost_estimate=pl.CostEstimate(flops=700_000, bytes_accessed=900_000, transcendentals=0),
    )(far_off(samples), valid, after, *map(far_off, consts))


def transform(filt, exact, first, twist, second):
    high = filt.astype(BF16)
    if exact:
        mid = jnp.dot(first[:, :64], high, preferred_element_type=F32) + jnp.dot(
            first[:, 128:], high, preferred_element_type=F32
        )
    else:
        low = (filt - high.astype(F32)).astype(BF16)
        mid = jnp.dot(
            first[...], jnp.concatenate([high, low, high], axis=0), preferred_element_type=F32
        )
    cos, sin = twist[:ROWS, :], twist[ROWS:, :]
    turned = []
    for sj in range(8):
        real = mid[:ROWS, sj * COLS : (sj + 1) * COLS]
        imag = mid[ROWS:, sj * COLS : (sj + 1) * COLS]
        turned.append(jnp.concatenate([real * cos + imag * sin, imag * cos - real * sin], axis=1))
    turned = jnp.concatenate(turned, axis=0)
    high = turned.astype(BF16)
    low = (turned - high.astype(F32)).astype(BF16)
    out = lax.dot_general(
        second[...],
        jnp.concatenate([high, low, high], axis=1),
        (((1,), (1,)), ((), ())),
        preferred_element_type=F32,
    )
    quarter = lax.broadcasted_iota(jnp.int32, (ROWS, COLS), 1) // ROWS
    spectra_of = []
    for part in range(2):
        for half in range(2):
            block = [
                out[(part * 4 + r) * 32 : (part * 4 + r + 1) * 32, half * 128 : (half + 1) * 128]
                for r in range(4)
            ]
            for b in range(4):
                moved = [
                    block[r] if r == b else pltpu.roll(block[r], 32 * ((r - b) % 4), 1)
                    for r in range(4)
                ]
                spec = jnp.where(
                    quarter < 2,
                    jnp.where(quarter == 0, moved[0], moved[1]),
                    jnp.where(quarter == 2, moved[2], moved[3]),
                )
                spectra_of.append(spec)
    return spectra_of


def own_kernel(past, after, part_sums, taps, first, twist, second, by_row):
    weights = [taps[k * ROWS : (k + 1) * ROWS, :] for k in range(TAPS)]
    columns = []
    for sig in range(2):
        both = []
        for part in range(2):
            index = part * 2 + sig
            frame = [
                past[(index * 3 + f) * 32 : (index * 3 + f + 1) * 32, :].astype(F32)
                for f in range(3)
            ]
            sums = [
                part_sums[(index * 4 + j) * 32 : (index * 4 + j + 1) * 32, :] for j in range(4)
            ]
            for j in range(3):
                for k in range(3 - j):
                    sums[j] = sums[j] + weights[k] * frame[j + k]
            both.append(sums)
        for j in range(4):
            columns.append(jnp.concatenate([both[0][j], both[1][j]], axis=0))
    filt = jnp.concatenate(columns, axis=1)
    for index, spec in enumerate(transform(filt, False, first, twist, second)):
        by_row[index * 32 : (index + 1) * 32, :] = spec.astype(BF16)


def own_spectra(past, *prepared):
    return pl.pallas_call(
        own_kernel,
        out_shape=jax.ShapeDtypeStruct((512, COLS), BF16),
        in_specs=[VMEM] * 7,
        out_specs=VMEM,
        compiler_params=pltpu.CompilerParams(vmem_limit_bytes=32 << 20),
        cost_estimate=pl.CostEstimate(flops=14_000_000_000, bytes_accessed=900_000, transcendentals=0),
    )(past, *prepared)


def pick_kernel(numbers, pieces, out):
    for k in range(STEPS):
        out[k * 16 : (k + 1) * 16, :] = pieces[pl.ds(pl.multiple_of(numbers[k] * 16, 16), 16), :]


def pick(numbers, pieces):
    return pl.pallas_call(
        pick_kernel,
        out_shape=jax.ShapeDtypeStruct((64, COLS), BF16),
        in_specs=[SMEM, VMEM],
        out_specs=VMEM,
        compiler_params=pltpu.CompilerParams(vmem_limit_bytes=32 << 20),
        cost_estimate=pl.CostEstimate(flops=0, bytes_accessed=150_000, transcendentals=0),
    )(numbers, pieces)


def filter_kernel(peers, numbers, picked, past, taps, out):
    weights = [
        jnp.broadcast_to(taps[pl.ds(numbers[1] + k * ROWS, 1), :], (8, COLS)) for k in range(TAPS)
    ]
    frame = lax.broadcasted_iota(jnp.int32, (8, COLS), 0) % 4
    now, before = picked[...].astype(F32), past[...].astype(F32)
    rows = []
    for start in range(0, 64, 8):
        mine, old = now[start : start + 8, :], before[start : start + 8, :]
        total = weights[3] * mine
        for k in range(3):
            moved = jnp.where(
                frame >= 3 - k, pltpu.roll(mine, 3 - k, 0), pltpu.roll(old, 7 - k, 0)
            )
            total = total + weights[k] * moved
        rows.append(total)
    rows = jnp.concatenate(rows, axis=0).astype(BF16)
    for peer in range(peers):
        out[peer * 64 : (peer + 1) * 64, :] = rows


def filter_tiles(numbers, picked, past, taps, peers):
    return pl.pallas_call(
        lambda *refs: filter_kernel(peers, *refs),
        out_shape=jax.ShapeDtypeStruct((peers * 64, COLS), BF16),
        in_specs=[SMEM, VMEM, VMEM, VMEM],
        out_specs=VMEM,
        compiler_params=pltpu.CompilerParams(vmem_limit_bytes=32 << 20),
        cost_estimate=pl.CostEstimate(flops=100_000, bytes_accessed=400_000, transcendentals=0),
    )(numbers, picked, past, taps)


def roots_kernel(both, first, twist, second, spectra, theirs):
    for core in range(2):
        for peer in range(16):
            start, at = (2 * peer + core) * 64, (core * 16 + peer) * 64
            theirs[start : start + 64, :] = both[at : at + 64, :].astype(F32)
    for k in range(STEPS):
        filt = jnp.concatenate(
            [
                jnp.concatenate(
                    [theirs[pl.ds(k * 16 + part * 8 + sj, ROWS, stride=64), :] for sj in range(8)],
                    axis=1,
                )
                for part in range(2)
            ],
            axis=0,
        )
        for index, spec in enumerate(transform(filt, True, first, twist, second)):
            at = (k * 16 + index) * 32
            spectra[at : at + 32, :] = spec


def root_spectra(both, *tables_near):
    return pl.pallas_call(
        roots_kernel,
        out_shape=jax.ShapeDtypeStruct((2048, COLS), F32),
        in_specs=[VMEM] * 4,
        out_specs=VMEM,
        scratch_shapes=[pltpu.VMEM((2048, COLS), F32)],
        compiler_params=pltpu.CompilerParams(vmem_limit_bytes=32 << 20),
        cost_estimate=pl.CostEstimate(flops=500_000_000, bytes_accessed=1_500_000, transcendentals=0),
    )(both, *tables_near)


def correlate_kernel(numbers, own, spectra, out, mine):
    count = numbers[0]
    weight = 1.0 / jnp.full((ROWS, COLS), count, jnp.int32).astype(F32)
    nothing = jnp.zeros((ROWS, COLS), F32)
    for j in range(4):
        scale = jnp.where(j < count, weight, nothing)
        for ps in range(4):
            rows = slice((ps * 4 + j) * 32, (ps * 4 + j + 1) * 32)
            mine[rows, :] = own[rows, :].astype(F32) * scale
    for k in range(STEPS):
        for s in range(2):
            for q in range(2):
                vis_real, vis_imag = nothing, nothing
                for j in range(4):
                    at = (s * 4 + j) * 32
                    a, b = mine[at : at + 32, :], mine[256 + at : 288 + at, :]
                    at = (k * 16 + q * 4 + j) * 32
                    real, imag = spectra[at : at + 32, :], spectra[256 + at : 288 + at, :]
                    vis_real = vis_real + (a * real + b * imag)
                    vis_imag = vis_imag + (b * real - a * imag)
                at = (k * 2 + s) * 64 + q
                out[pl.ds(at, ROWS, stride=2), :] = vis_real
                out[pl.ds(512 + at, ROWS, stride=2), :] = vis_imag


def correlate(numbers, own, spectra):
    return pl.pallas_call(
        correlate_kernel,
        out_shape=jax.ShapeDtypeStruct((1024, COLS), F32),
        in_specs=[SMEM, VMEM, VMEM],
        out_specs=VMEM,
        scratch_shapes=[pltpu.VMEM((512, COLS), F32)],
        compiler_params=pltpu.CompilerParams(vmem_limit_bytes=32 << 20),
        cost_estimate=pl.CostEstimate(flops=4_000_000, bytes_accessed=1_500_000, transcendentals=0),
    )(numbers, own, spectra)


def local(samples, valid_spectra, root_blocks):
    blocks, places = lax.axis_size("tm"), lax.axis_size("stn")
    onward = [(b, b + 1) for b in range(blocks - 1)]
    same_core = [[2 * p + c for p in range(places // 2)] for c in range(2)]
    by_tile, roots = tiles_of(samples, root_blocks)
    pieces = lax.all_to_all(by_tile, "stn", 0, 0, tiled=True)
    picked = pick(roots, pieces)
    picked_past = lax.ppermute(picked, "tm", onward)
    part_sums, tails, taps, first, twist, second, numbers = ready(samples, valid_spectra, picked)
    past = lax.ppermute(tails, "tm", onward)
    tiles = filter_tiles(numbers, picked, picked_past, taps, places // 2)
    near = lax.all_to_all(tiles, "stn", 0, 0, axis_index_groups=same_core, tiled=True)
    pairs = [[2 * p, 2 * p + 1] for p in range(places // 2)]
    both = lax.all_gather(near, "stn", axis_index_groups=pairs)
    roots_near = root_spectra(both.reshape(-1, COLS), first, twist, second)
    own = own_spectra(past, roots_near, part_sums, taps, first, twist, second)
    vis = correlate(numbers, own, roots_near)
    vis = vis.reshape(2, STEPS, 2, 32, 2, COLS).transpose(0, 1, 2, 4, 3, 5)
    return vis.reshape(1, 2, STEPS, 2, 2, 32 * COLS)


def solution(mesh):
    return jax.shard_map(
        local,
        mesh=mesh,
        in_specs=(P(None, "stn", "tm", None), P("tm"), P()),
        out_specs=P("tm", None, None, "stn", None, None),
        check_vma=False,
    )
```

time: 63.9 us -> 53.1 us (0.83)
  the two profiles are of different devices: /device:TPU:257 before, /device:TPU:707 now
where the time goes in v4:
time: 53.1 us; the launch traced here: 52.7 us
  waiting for transfers between devices  17.2 us (32%)
  blocking collectives  16.5 us (31%)
  starting transfers between devices  11.8 us (22%)
  Pallas kernels  6.57 us (12%)
  between operations  0.7 us (1%)
    all_to_all x1, blocking collectives, local(): pieces = lax.all_to_all(by_tile, 'stn', 0, 0, tiled=True)  13.3 us
    ppermute x1, waiting for transfers between devices, local(): past = lax.ppermute(tails, 'tm', onward)  6.81 us
    all_to_all x1, starting transfers between devices, local(): lax.all_to_all(tiles, 'stn', 0, 0, axis_index_groups=same_core, tiled=True)  6.69 us
    ppermute x1, waiting for transfers between devices, local(): picked_past = lax.ppermute(picked, 'tm', onward)  5.41 us
    all_to_all x1, waiting for transfers between devices, local(): lax.all_to_all(tiles, 'stn', 0, 0, axis_index_groups=same_core, tiled=True)  4.94 us
    ppermute x1, starting transfers between devices, local(): picked_past = lax.ppermute(picked, 'tm', onward)  3.19 us
    all_gather x1, blocking collectives, local(): both = lax.all_gather(near, 'stn', axis_index_groups=pairs)  3.18 us
    pallas_call x1, Pallas kernels, root_spectra(): pl.pallas_call(roots_kernel, out_shape=jax.ShapeDtypeStruct((2048, COLS),...  1.99 us
  transfers between devices with their start and end apart: 3, of which 3 were waited for; matrix products, arithmetic and copies ran while one was open for 0% of the time, Pallas kernels for 6%

profile of v4, /device:TPU:707, one launch (start us, length us, event | category | flops | bytes accessed | tf_op | source)
XLA Modules:
  0.0 52.7 jit_solution(457157370568569926)
XLA Ops:
  0.0 0.9 %shard_map.73 = (bf16[512,128]{1,0:T(8,128)(2,1)S(1)}, s32[5]{0:T(128)S(4)}) custom-call(bf16[2,2,4,4096]{3,2,1,0:T(4,128)(2,1)} %samples.3, s32[4]{0:T(128)} %roots.1), custom_call_target="tpu_custom_call" | custom-call | bytes 600000 | tf_op jit(solution)/shard_map/pallas_call | solution.py:92
  0.9 13.3 %all_to_all.20 = bf16[32,16,128]{2,1,0:T(8,128)(2,1)S(1)} all-to-all(bf16[32,16,128]{2,1,0:T(8,128)(2,1)S(1)} %bitcast.12), channel_id=1, replica_groups=mesh['stn'=32,'tm'=24] {'stn'}, dimensions={0} | all-to-all | bytes 262144 | tf_op jit(solution)/shard_map/all_to_all | solution.py:372
  14.2 3.2 %collective-permute-start.1 = (bf16[64,128]{1,0:T(8,128)(2,1)S(1)}, bf16[64,128]{1,0:T(8,128)(2,1)S(1)}, u32[]{:S(2)}, u32[]{:S(2)}) collective-permute-start(bf16[64,128]{1,0:T(8,128)(2,1)S(1)} %shard_map.74.after.refs_1_), channel_id=1, source_target_pairs={{0,1},{1,2},{2,3},{3,4},{4,5},{5,6},{6,7},{7,8},{8,9},{9,10},{10,1... | collective-permute-start | bytes 49160 | tf_op jit(solution)/shard_map/ppermute | solution.py:374
  18.1 1.2 %shard_map.75 = (f32[512,128]{1,0:T(8,128)S(1)}, bf16[384,128]{1,0:T(8,128)(2,1)S(1)}, f32[128,128]{1,0:T(8,128)S(1)}, bf16[64,192]{1,0:T(8,128)(2,1)S(1)}, f32[...) custom-call(bf16[2,2,4,4096]{3,2,1,0:T(4,128)(2,1)} %samples.3, s32[1]{0:T(128)S(6)} %copy.10.valid, ...), custom_call_target="tpu_custom_call" | custom-call | flops 700000 | bytes 900000 | tf_op jit(solution)/shard_map/pallas_call | solution.py:145
  19.3 5.4 %collective-permute-done.1.refs_2_ = bf16[64,128]{1,0:T(8,128)(2,1)S(1)} collective-permute-done((bf16[64,128]{1,0:T(8,128)(2,1)S(1)}, bf16[64,128]{1,0:T(8,128)(2,1)S(1)}, u32[]{:S(2)}, u32[]{:S(2)}) %collective-permute-start.1) | collective-permute-done | bytes 16416 | tf_op jit(solution)/shard_map/ppermute | solution.py:374
  24.7 0.7 %shard_map.76 = bf16[1024,128]{1,0:T(8,128)(2,1)} custom-call(s32[2]{0:T(128)S(4)} %get-tuple-element.16.refs_0_.numbers, bf16[64,128]{1,0:T(8,128)(2,1)S(1)} %shard_map.74.after.refs_1_, bf16[64,128]{1,0:T(8,128)(2,1)S(1)} %collective-permute-done.1.refs_2_, f32[128,128]{1,0:T(8,128)S(1)} %get-tuple-element.18.refs_3_.taps), custom_call_target="tpu_custom_call" | custom-call | flops 100000 | bytes 400000 | tf_op jit(solution)/shard_map/pallas_call | solution.py:287
  25.4 6.7 %all-to-all-start.1 = ((bf16[16,64,128]{2,1,0:T(8,128)(2,1)}), bf16[16,64,128]{2,1,0:T(8,128)(2,1)S(1)}, u32[]{:S(2)}, u32[]{:S(2)}) async-start(bf16[16,64,128]{2,1,0:T(8,128)(2,1)} %bitcast.2), calls=%async_computation.1 | async-start | bytes 524288 | tf_op jit(solution)/shard_map/all_to_all | solution.py:378
  32.1 1.9 %collective-permute-start = (bf16[384,128]{1,0:T(8,128)(2,1)S(1)}, bf16[384,128]{1,0:T(8,128)(2,1)S(1)}, u32[]{:S(2)}, u32[]{:S(2)}) collective-permute-start(bf16[384,128]{1,0:T(8,128)(2,1)S(1)} %get-tuple-element.17), channel_id=1, source_target_pairs={{0,1},{1,2},{2,3},{3,4},{4,5},{5,6},{6,7},{7,8},{8,9},{9,10},{10,1... | collective-permute-start | bytes 294920 | tf_op jit(solution)/shard_map/ppermute | solution.py:376
  34.0 4.9 %all-to-all-done.1 = bf16[16,64,128]{2,1,0:T(8,128)(2,1)S(1)} async-done(((bf16[16,64,128]{2,1,0:T(8,128)(2,1)}), bf16[16,64,128]{2,1,0:T(8,128)(2,1)S(1)}, u32[]{:S(2)}, u32[]{:S(2)}) %all-to-all-start.1) | async-done | bytes 262176 | tf_op jit(solution)/shard_map/all_to_all | solution.py:378
  39.0 3.2 %all_gather.7 = bf16[2,1024,128]{2,1,0:T(8,128)(2,1)S(1)} all-gather(bf16[1,1024,128]{2,1,0:T(8,128)(2,1)S(1)} %bitcast.13), channel_id=1, replica_groups={{0,24},{48,72},{96,120},{144,168},{192,216},{240,264},{288,312},{336,36..., dimensions={0}, use_global_device_ids=true | all-gather | bytes 786432 | tf_op jit(solution)/shard_map/all_gather | solution.py:380
  42.2 2.0 %shard_map.77.after.spectra = f32[2048,128]{1,0:T(8,128)S(1)} custom-call(bf16[2048,128]{1,0:T(8,128)(2,1)S(1)} %bitcast.10, bf16[64,192]{1,0:T(8,128)(2,1)S(1)} %get-tuple-element.19.first, f32[64,128]{1,0:T(8,128)S(1)} %get-tuple-element.20.twist, bf16[256,768]{1,0:T(8,128)(2,1)S(1)} %get-tuple-element.21.second), custom_call_target="tpu_custom_call" | custom-call | flops 500000000 | bytes 1500000 | tf_op jit(solution)/shard_map/pallas_call | solution.py:319
  44.2 6.8 %collective-permute-done.past = bf16[384,128]{1,0:T(8,128)(2,1)S(1)} collective-permute-done((bf16[384,128]{1,0:T(8,128)(2,1)S(1)}, bf16[384,128]{1,0:T(8,128)(2,1)S(1)}, u32[]{:S(2)}, u32[]{:S(2)}) %collective-permute-start) | collective-permute-done | bytes 98336 | tf_op jit(solution)/shard_map/ppermute | solution.py:376
  51.0 0.6 %shard_map.78.own = bf16[512,128]{1,0:T(8,128)(2,1)S(1)} custom-call(bf16[384,128]{1,0:T(8,128)(2,1)S(1)} %collective-permute-done.past, f32[2048,128]{1,0:T(8,128)S(1)} %shard_map.77.after.spectra, f32[512,128]{1,0:T(8,128)S(1)} %get-tuple-element.22.part_sums, f32[128,128]{1,0:T(8,128)S(1)} %get-tuple-element.18.refs_3_.taps, ...), custom_call_target="tpu_custom_call" | custom-call | flops 14000000000 | bytes 900000 | tf_op jit(solution)/shard_map/pallas_call | solution.py:239
  51.6 1.1 %shard_map.79 = f32[1024,128]{1,0:T(8,128)} custom-call(s32[2]{0:T(128)S(4)} %get-tuple-element.16.refs_0_.numbers, bf16[512,128]{1,0:T(8,128)(2,1)S(1)} %shard_map.78.own, f32[2048,128]{1,0:T(8,128)S(1)} %shard_map.77.after.spectra), custom_call_target="tpu_custom_call" | custom-call | flops 4000000 | bytes 1500000 | tf_op jit(solution)/shard_map/pallas_call | solution.py:356
  (1 shorter events, 0.0 us)
Async XLA Ops:
  14.2 10.5 %collective-permute-start.1 = (bf16[64,128]{1,0:T(8,128)(2,1)S(1)}, bf16[64,128]{1,0:T(8,128)(2,1)S(1)}, u32[]{:S(2)}, u32[]{:S(2)}) collective-permute-start(bf16[64,128]{1,0:T(8,128)(2,1)S(1)} %shard_map.74.after.refs_1_), channel_id=1, source_target_pairs={{0,1},{1,2},{2,3},{3,4},{4,5},{5,6},{6,7},{7,8},{8,9},{9,10},{10,1... | collective-permute-start | bytes 49160 | tf_op jit(solution)/shard_map/ppermute | solution.py:374
  25.4 13.5 %all-to-all-start.1 = ((bf16[16,64,128]{2,1,0:T(8,128)(2,1)}), bf16[16,64,128]{2,1,0:T(8,128)(2,1)S(1)}, u32[]{:S(2)}, u32[]{:S(2)}) async-start(bf16[16,64,128]{2,1,0:T(8,128)(2,1)} %bitcast.2), calls=%async_computation.1 | async-start | bytes 524288 | tf_op jit(solution)/shard_map/all_to_all | solution.py:378
  32.1 18.9 %collective-permute-start = (bf16[384,128]{1,0:T(8,128)(2,1)S(1)}, bf16[384,128]{1,0:T(8,128)(2,1)S(1)}, u32[]{:S(2)}, u32[]{:S(2)}) collective-permute-start(bf16[384,128]{1,0:T(8,128)(2,1)S(1)} %get-tuple-element.17), channel_id=1, source_target_pairs={{0,1},{1,2},{2,3},{3,4},{4,5},{5,6},{6,7},{7,8},{8,9},{9,10},{10,1... | collective-permute-start | bytes 294920 | tf_op jit(solution)/shard_map/ppermute | solution.py:376
